TPU v7x, 512 devices: a whole 4x8x8 slice. The times are simulated.
512 devices in a mesh: row: 32 (over z_lo, y), col: 16 (over z_hi, x, core).
Axes of the slice: x: 4, y: 8, z: 8 (z_hi: 2, z_lo: 4; z = z_hi * 4 + z_lo), core: 2. Of those that a mesh axis runs over, the one named last changes fastest.
Arguments:
- center: bfloat16 [2048, 8192], P('col', 'row'), may hold values from -6 to 6
- radius: bfloat16 [2048, 8192], P('col', 'row'), may hold values from 0.049804688 to 1
- grad_center: bfloat16 [2048, 8192], P('row', 'col'), may hold values from -6 to 6
- grad_radius: bfloat16 [2048, 8192], P('row', 'col'), may hold values from -6 to 6
- weight: bfloat16 [8192, 8192], P('row', 'col'), may hold values from -0.0625 to 0.0625
- active: int32 [2048, 8192], P('col', 'row'), may hold values 0 or 1
Outputs:
- center_in: float32 [2048, 8192], P('col', 'row')
- radius_in: float32 [2048, 8192], P('col', 'row')
- weight_grad: float32 [8192, 8192], P('row', 'col')
All inputs are finite; a program needn't handle non-finite values. No bound on the sum of `active` on one device may be relied on, other than what follows from the above.
Results may differ from a plain program's by a relative error of at most 0.0003.
Values may be sent and summed in bfloat16 or wider, within the bound.
A program may use at most 64 MiB of HBM per device.

v0:
```python
import jax
import jax.numpy as jnp
from jax import lax
from jax.sharding import PartitionSpec as P


def on_device(center, radius, grad_center, grad_radius, weight, active):
    magnitude = jnp.abs(weight)
    stacked = jnp.stack((grad_center, grad_radius))
    inputs = lax.all_gather(jnp.stack((center, radius)), "col", axis=1, tiled=True)
    contract_out = (((1,), (1,)), ((), ()))
    contract_tok = (((0,), (0,)), ((), ()))
    total_tokens = inputs.shape[1]
    panels = lax.all_gather(stacked, "row", axis=1, tiled=True)
    through_center = lax.dot_general(
        panels[0], weight, contract_out, preferred_element_type=jnp.float32
    )
    through_radius = lax.dot_general(
        panels[1], magnitude, contract_out, preferred_element_type=jnp.float32
    )
    partial_terms = jnp.stack((through_center, through_radius))
    center_acc = lax.dot_general(
        inputs[0], panels[0], contract_tok, preferred_element_type=jnp.float32
    )
    radius_acc = lax.dot_general(
        inputs[1], panels[1], contract_tok, preferred_element_type=jnp.float32
    )
    center_acc, radius_acc = (center_acc, radius_acc)
    summed = lax.psum_scatter(partial_terms, "col", scatter_dimension=1, tiled=True)
    gating = active.astype(jnp.float32)
    center_in = gating * summed[0]
    radius_in = gating * summed[1]
    scale_factor = jnp.float32(1.0) / jnp.sqrt(jnp.float32(total_tokens))
    weight_grad = (center_acc + jnp.sign(weight).astype(jnp.float32) * radius_acc) * scale_factor
    return (center_in, radius_in, weight_grad)


def solution(mesh):
    in_specs = (
        P("col", "row"),
        P("col", "row"),
        P("row", "col"),
        P("row", "col"),
        P("row", "col"),
        P("col", "row"),
    )
    out_specs = (P("col", "row"), P("col", "row"), P("row", "col"))
    return jax.shard_map(
        on_device, mesh=mesh, in_specs=in_specs, out_specs=out_specs, check_vma=False
    )
```

profile of v0, /device:TPU:8, one launch (start us, length us, event | category | flops | bytes accessed | tf_op | source)
XLA Modules:
  0.0 365.3 jit_solution(8215343059179930053)
XLA Ops:
  7.2 0.0 all-gather.3.cloned.1.call-start
  7.2 1.5 pad_maximum_fusion.1
  8.8 0.0 all-gather.3.cloned.1.call-update
  8.8 0.0 all-gather.5.cloned.1.call-start
  8.8 1.5 pad_maximum_fusion.2
  10.4 0.0 all-gather.5.cloned.1.call-update
  10.4 0.0 copy-start.1
  10.4 0.0 reduce-scatter.2.cloned.1.call-start
  10.5 163.6 %all-gather.3.cloned.1.call-done = bf16[2,2048,512]{2,1,0:T(8,128)(2,1)} async-done(((bf16[2,64,512]{2,1,0:T(8,128)(2,1)}), bf16[2,2048,512]{2,1,0:T(8,128)(2,1)}) %all-gather.3.cloned.1.call-update) | async-done | bytes 4194320 | tf_op jit(solution)/shard_map/all_gather | solution.py:14
  174.1 0.0 copy-start
  174.1 2.5 convolution_bitcast_fusion.1
  176.6 0.0 copy-done.1
  176.6 0.4 copy-done
  177.0 0.7 convolution_bitcast_fusion
  177.7 2.2 pad_maximum_fusion
  180.0 0.0 reduce-scatter.2.cloned.1.call-update
  180.0 62.9 %all-gather.5.cloned.1.call-done = bf16[2,2048,256]{2,1,0:T(8,128)(2,1)} async-done(((bf16[2,128,256]{2,1,0:T(8,128)(2,1)}), bf16[2,2048,256]{2,1,0:T(8,128)(2,1)}) %all-gather.5.cloned.1.call-update) | async-done | bytes 2097168 | tf_op jit(solution)/shard_map/all_gather | solution.py:10
  242.9 2.8 fusion
  245.7 0.0 copy-done.3
  245.7 0.0 copy-start.2
  245.7 3.2 fusion.4
  248.9 108.1 %reduce-scatter.2.cloned.1.call-done = f32[2,128,256]{2,1,0:T(8,128)} async-done(((f32[2,2048,256]{2,1,0:T(8,128)}), f32[2,128,256]{2,1,0:T(8,128)}) %reduce-scatter.2.cloned.1.call-update) | async-done | bytes 262160 | tf_op jit(solution)/shard_map/reduce_scatter | solution.py:29
  357.1 0.0 copy-done.2
  357.1 1.7 fusion.6
  (1 shorter events, 0.0 us)
Async XLA Ops:
  7.2 166.9 %all-gather.3.cloned.1.call-start = ((), (), s32[]{:S(2)}) async-start(), calls=%async_computation.1 | async-start | bytes 4325376 | tf_op jit(solution)/shard_map/all_gather | solution.py:14
  8.8 234.1 %all-gather.5.cloned.1.call-start = ((), (), s32[]{:S(2)}) async-start(), calls=%async_computation.3 | async-start | bytes 2228224 | tf_op jit(solution)/shard_map/all_gather | solution.py:10
  10.4 166.2 %copy-start.1 = (bf16[256,512]{1,0:T(8,128)(2,1)S(1)}, bf16[256,512]{1,0:T(8,128)(2,1)}, u32[]{:S(2)}) copy-start(bf16[256,512]{1,0:T(8,128)(2,1)} %param.10) | copy-start | bytes 786436
  10.4 346.6 %reduce-scatter.2.cloned.1.call-start = ((), (), s32[]{:S(2)}) async-start(), calls=%async_computation.2 | async-start | bytes 4456448 | tf_op jit(solution)/shard_map/reduce_scatter | solution.py:29
  174.1 2.9 copy-start
  242.9 2.8 copy-start.3
  245.7 111.3 %copy-start.2 = (s32[128,256]{1,0:T(8,128)S(1)}, s32[128,256]{1,0:T(8,128)}, u32[]{:S(2)}) copy-start(s32[128,256]{1,0:T(8,128)} %param.11) | copy-start | bytes 393220
Sparse Core Ops, SparseCore 0:
  10.7 163.3 all-gather.2
  178.0 64.8 all-gather.4
  247.8 109.1 reduce-scatter.1
where the time goes:
time: 366 us; the launch traced here: 365 us
  waiting for transfers between devices  335 us (92%)
  between operations  13.8 us (4%)
  matrix products  9.2 us (3%)
  other arithmetic  7.01 us (2%)
    all_gather x1, waiting for transfers between devices, on_device(): panels = lax.all_gather(stacked, 'row', axis=1, tiled=True)  164 us
    reduce_scatter x1, waiting for transfers between devices, on_device(): lax.psum_scatter(partial_terms, 'col', scatter_dimension=1, tiled=True)  108 us
    all_gather x1, waiting for transfers between devices, on_device(): lax.all_gather(jnp.stack((center, radius)), 'col', axis=1, tiled=True)  62.9 us
  transfers between devices with their start and end apart: 3, of which 3 were waited for; matrix products, arithmetic and copies ran while one was open for 4% of the time, Pallas kernels for 0%

commit v1 on v0

v1 whole, which is shorter than its diff:
```python
import functools

import jax
import jax.numpy as jnp
from jax import lax
from jax.experimental import pallas as pl
from jax.experimental.pallas import tpu as pltpu
from jax.sharding import PartitionSpec as P

MESH = pl.DeviceIdType.MESH
F32 = jnp.float32
BF16 = jnp.bfloat16


def dot_nt(a, b):
    return lax.dot_general(a, b, (((1,), (1,)), ((), ())), preferred_element_type=F32)


def dot_tn(a, b):
    return lax.dot_general(a, b, (((0,), (0,)), ((), ())), preferred_element_type=F32)


def kernel(
    scale,
    ctr, rad, gc, gr, w, act,
    oc, orad, ow,
    G, C, Wb, Wa, S, R, Zs, F, acc, wsend, wrecv,
    ring_s, ring_r, own_s, own_r, z_s, z_r, sib_s, sib_r, cin_s, cin_r, x_s, x_r, f_s, f_r,
):
    row, col = lax.axis_index("row"), lax.axis_index("col")
    zl, y = row // 8, row % 8
    zh, x, k = col // 8, (col % 8) // 2, col % 2
    z1, z0 = zl // 2, zl % 2
    mid = (z0 + z1) % 2

    def dev(x=x, y=y, zl=zl, zh=zh, k=k):
        return (zl * 8 + y, zh * 8 + x * 2 + k)

    def flip(j):
        return ((z1 + j // 2) % 2) * 2 + (z0 + j % 2) % 2

    order = [0, 1, 2 + mid, 3 - mid]
    ok = 1 - k
    up, down = (y + 1) % 8, (y + 7) % 8

    def rows32(i):
        return pl.ds(pl.multiple_of(i * 32, 32), 32)

    def at_y(off):
        return (y + off + 8) % 8

    sent = []

    def copy(src, dst, ssem, rsem, to):
        return pltpu.make_async_remote_copy(
            src_ref=src, dst_ref=dst, send_sem=ssem, recv_sem=rsem, device_id=to, device_id_type=MESH
        )

    def send(c, cond=None):
        if cond is None:
            c.start()
        else:
            pl.when(cond)(c.start)
        sent.append((c, cond))

    zrows = rows32(zl)
    G[y, 0, k, zrows] = gc[rows32(k)]
    G[y, 1, k, zrows] = gr[rows32(k)]
    cz = rows32(zh * 2 + x // 2)
    cy = (x % 2) * 4 + k * 2
    C[pl.ds(cy, 2), 0, cz] = ctr[:, rows32(k)]
    C[pl.ds(cy, 2), 1, cz] = rad[:, rows32(k)]

    peers = [dev(y=up), dev(y=down), dev(k=ok), dev(zh=1 - zh), dev(zh=1 - zh, k=ok)]
    peers += [dev(zl=flip(j)) for j in (1, 2, 3)]
    peers += [dev(x=(x + i) % 4) for i in (1, 2, 3)]
    bar = pltpu.get_barrier_semaphore()
    for p in peers:
        pl.semaphore_signal(bar, inc=1, device_id=p, device_id_type=MESH)
    pl.semaphore_wait(bar, len(peers))

    def own_y(part, kc):
        blk = G.at[y, :, kc, zrows]
        for i, to in enumerate((up, down)):
            send(copy(blk, blk, own_s.at[part, i], own_r.at[part, i], dev(y=to)))

    def own_z(part, kc):
        blk = G.at[y, :, kc, zrows]
        for i in (1, 2, 3):
            j = order[i]
            send(copy(blk, blk, z_s.at[part, i - 1], z_r.at[part, j - 1], dev(zl=flip(j))))

    own_y(0, k)
    sib = dev(k=ok)
    gsib = [copy(ref.at[rows32(ok)], G.at[y, a, k, zrows], sib_s.at[a], sib_r.at[a], sib) for a, ref in enumerate((gc, gr))]
    csib = [
        copy(ref.at[:, rows32(ok)], C.at[pl.ds(cy, 2), a, cz], sib_s.at[2 + a], sib_r.at[2 + a], sib)
        for a, ref in enumerate((ctr, rad))
    ]
    wsib = copy(w, Wb.at[k], sib_s.at[4], sib_r.at[4], sib)
    for c in gsib:
        send(c)
    own_z(0, k)
    for c in csib:
        send(c)
    send(wsib)
    Wb[k] = w[...]
    Wa[k] = jnp.abs(w[...])
    for c in gsib:
        c.wait_recv()
    own_y(1, ok)
    own_z(1, ok)
    for c in csib:
        c.wait_recv()

    def cin(zh_):
        return C.at[pl.ds((x % 2) * 4, 4), :, rows32(zh_ * 2 + x // 2)]

    def cin_x(zh_, part):
        for i in (1, 2, 3):
            blk = cin(zh_)
            send(copy(blk, blk, cin_s.at[part, i - 1], cin_r.at[part, i - 1], dev(x=(x + i) % 4)))

    far = copy(cin(zh), cin(zh), cin_s.at[2, 0], cin_r.at[2, 0], dev(zh=1 - zh))
    send(far)
    cin_x(zh, 0)

    def ring_copy(j, d, up_dir):
        ys = at_y(-d) if up_dir else at_y(d)
        i = 0 if up_dir else 1
        zr = rows32(flip(order[j]))
        if d < 3:
            blk = G.at[ys, :, :, zr]
        else:
            blk = G.at[ys, i, :, zr]
        return copy(blk, blk, ring_s.at[i, d, j], ring_r.at[i, d, j], dev(y=up if up_dir else down))

    def arrive(j, d):
        if d == 0:
            if j:
                jj = order[j]
                blk = G.at[y, :, k, zrows]
                for part in (0, 1):
                    copy(blk, blk, z_s.at[part, 0], z_r.at[part, jj - 1], dev()).wait_recv()
        elif d == 1 and j == 0:
            blk = G.at[y, :, k, zrows]
            for part in (0, 1):
                for i in (0, 1):
                    copy(blk, blk, own_s.at[part, i], own_r.at[part, i], dev()).wait_recv()
        else:
            ring_copy(j, d - 1, True).wait_recv()
            ring_copy(j, d - 1, False).wait_recv()

    def step(j, d):
        arrive(j, d)
        if d < 4:
            send(ring_copy(j, d, True))
            send(ring_copy(j, d, False))

    def x_copy(yb, g):
        xd = g * 2 + yb // 4
        return copy(S.at[yb, :, :, g], R.at[x, yb % 4], x_s.at[yb, g], x_r.at[x, yb % 4], dev(x=xd)), xd != x

    def through(off):
        yb = at_y(off)
        for a, m in ((0, Wb), (1, Wa)):
            p = dot_nt(G[yb, a, 0], m[0]) + dot_nt(G[yb, a, 1], m[1])
            S[yb, a] = p.reshape(2, 2, 32, 256)
        for g in (0, 1):
            c, cond = x_copy(yb, g)
            send(c, cond)

    def grad(off, first=False):
        yb = at_y(off)
        for a in (0, 1):
            for kc in (0, 1):
                t = dot_tn(C[yb, a], G[yb, a, kc])
                if first:
                    acc[a, kc] = t
                else:
                    acc[a, kc] += t

    def f_send(src, to, slot_s, slot_r):
        return copy(src, F.at[zh, k, slot_r], f_s.at[slot_s], f_r.at[zh, k, slot_r], to)

    def owner(off):
        yb = at_y(off)
        yq = yb % 4
        mine = yb // 4 == x % 2
        to_core, yy = yq // 2, yq % 2

        @pl.when(mine)
        def _():
            g = x // 2
            for i in (1, 2, 3):
                xs = (x + i) % 4
                copy(S.at[yb, :, :, g], R.at[xs, yq], x_s.at[yb, g], x_r.at[xs, yq], dev()).wait_recv()
            for a in (0, 1):
                for h in (zh, 1 - zh):
                    t = S[yb, a, h, g]
                    for i in (1, 2, 3):
                        t = t + R[(x + i) % 4, yq, a, h]
                    Zs[yq, h, a] = t

        send(f_send(Zs.at[yq, 1 - zh], dev(zh=1 - zh, k=to_core), yq, yy), mine)
        here = Zs.at[yq, zh]
        send(f_send(here, dev(k=ok), 4 + yy, yy), mine & (to_core != k))

        @pl.when(mine & (to_core == k))
        def _():
            F[zh, k, yy] = Zs[yq, zh]

    step(1, 0)
    step(0, 1)
    step(2, 0)
    step(3, 0)
    wsib.wait_recv()
    Wa[ok] = jnp.abs(Wb[ok])
    through(0)
    step(1, 1)
    far_in = copy(cin(1 - zh), cin(1 - zh), cin_s.at[2, 0], cin_r.at[2, 0], dev())
    far_in.wait_recv()
    cin_x(1 - zh, 1)
    step(2, 1)
    step(3, 1)
    through(1)
    through(-1)
    step(0, 2)
    owner(0)
    step(1, 2)
    for part, h in ((0, zh), (1, 1 - zh)):
        for i in (1, 2, 3):
            copy(cin(h), cin(h), cin_s.at[part, i - 1], cin_r.at[part, i - 1], dev()).wait_recv()
    grad(0, True)
    step(2, 2)
    grad(1)
    step(3, 2)
    grad(-1)
    through(2)
    through(-2)
    step(0, 3)
    owner(1)
    owner(-1)
    step(1, 3)
    grad(2)
    step(2, 3)
    grad(-2)
    step(3, 3)
    through(3)
    through(-3)
    owner(2)
    owner(-2)
    grad(3)
    grad(-3)
    for j in range(4):
        step(j, 4)
    through(4)
    owner(3)
    owner(-3)
    grad(4)

    def combined(kc):
        wf = Wb[kc].astype(F32)
        sgn = jnp.where(wf > 0, 1.0, jnp.where(wf < 0, -1.0, 0.0))
        return acc[0, kc] + sgn * acc[1, kc]

    wsend[...] = combined(ok)
    wg = copy(wsend, wrecv, sib_s.at[5], sib_r.at[5], sib)
    send(wg)
    ow[...] = combined(k)
    owner(4)
    wg.wait_recv()
    ow[...] = (ow[...] + wrecv[...]) * scale

    for yy in (0, 1):
        for h, kk in ((zh, ok), (1 - zh, k), (1 - zh, ok)):
            copy(Zs.at[0, 0], F.at[h, kk, yy], f_s.at[0], f_r.at[h, kk, yy], dev()).wait_recv()
    for a, o in ((0, oc), (1, orad)):
        for yy in (0, 1):
            for kk in (0, 1):
                gate = act[yy, pl.ds(kk * 32, 32)].astype(F32)
                o[yy, pl.ds(kk * 32, 32)] = gate * (F[0, kk, yy, a] + F[1, kk, yy, a])
    for c, cond in sent:
        if cond is None:
            c.wait_send()
        else:
            pl.when(cond)(c.wait_send)


def on_device(center, radius, grad_center, grad_radius, weight, active):
    vm = pl.BlockSpec(memory_space=pltpu.VMEM)
    dma = pltpu.SemaphoreType.DMA
    oc, orad, ow = pl.pallas_call(
        functools.partial(kernel, 2048.0 ** -0.5),
        out_shape=(
            jax.ShapeDtypeStruct((2, 64, 256), F32),
            jax.ShapeDtypeStruct((2, 64, 256), F32),
            jax.ShapeDtypeStruct((256, 512), F32),
        ),
        in_specs=[vm] * 6,
        out_specs=(vm,) * 3,
        scratch_shapes=[
            pltpu.VMEM((8, 2, 2, 128, 512), BF16),
            pltpu.VMEM((8, 2, 128, 256), BF16),
            pltpu.VMEM((2, 256, 512), BF16),
            pltpu.VMEM((2, 256, 512), BF16),
            pltpu.VMEM((8, 2, 2, 2, 32, 256), F32),
            pltpu.VMEM((4, 4, 2, 2, 32, 256), F32),
            pltpu.VMEM((4, 2, 2, 32, 256), F32),
            pltpu.VMEM((2, 2, 2, 2, 32, 256), F32),
            pltpu.VMEM((2, 2, 256, 512), F32),
            pltpu.VMEM((256, 512), F32),
            pltpu.VMEM((256, 512), F32),
            dma((2, 4, 4)), dma((2, 4, 4)),
            dma((2, 2)), dma((2, 2)),
            dma((2, 3)), dma((2, 3)),
            dma((6,)), dma((6,)),
            dma((3, 3)), dma((3, 3)),
            dma((8, 2)), dma((4, 4)),
            dma((6,)), dma((2, 2, 2)),
        ],
        compiler_params=pltpu.CompilerParams(collective_id=0, has_side_effects=True, vmem_limit_bytes=48 * 2**20),
        cost_estimate=pl.CostEstimate(flops=2 * 2**30, bytes_accessed=2**21, transcendentals=0),
        name="bounds",
    )(
        center.reshape(2, 64, 256), radius.reshape(2, 64, 256), grad_center, grad_radius, weight, active.reshape(2, 64, 256)
    )
    return oc.reshape(128, 256), orad.reshape(128, 256), ow


def solution(mesh):
    in_specs = (
        P("col", "row"),
        P("col", "row"),
        P("row", "col"),
        P("row", "col"),
        P("row", "col"),
        P("col", "row"),
    )
    out_specs = (P("col", "row"), P("col", "row"), P("row", "col"))
    return jax.shard_map(
        on_device, mesh=mesh, in_specs=in_specs, out_specs=out_specs, check_vma=False
    )
```

time: 366 us -> 90.2 us (0.25)
  the two profiles are of different devices: /device:TPU:8 before, /device:TPU:10 now
where the time goes in v1:
time: 90.2 us; the launch traced here: 89.9 us
  Pallas kernels  81.9 us (91%)
  local copies, waits for them, and re-layouts  7.31 us (8%)
    pallas_call x1, Pallas kernels, on_device(): pl.pallas_call(functools.partial(kernel, 2048.0 ** (-0.5)), out_shape=(ja...  81.9 us
    unnamed x15, local copies, waits for them, and re-layouts  7.31 us

profile of v1, /device:TPU:10, one launch (start us, length us, event | category | flops | bytes accessed | tf_op | source)
XLA Modules:
  0.0 89.9 jit_solution(1797189861989394317)
XLA Ops:
  0.6 0.0 copy-start
  0.6 0.9 %copy-done = bf16[256,512]{1,0:T(8,128)(2,1)S(1)} copy-done((bf16[256,512]{1,0:T(8,128)(2,1)S(1)}, bf16[256,512]{1,0:T(8,128)(2,1)}, u32[]{:S(2)}) %copy-start) | copy-done | bytes 262168
  1.6 0.0 copy-start.1
  1.6 0.9 %copy-done.1 = s32[128,256]{1,0:T(8,128)S(1)} copy-done((s32[128,256]{1,0:T(8,128)S(1)}, s32[128,256]{1,0:T(8,128)}, u32[]{:S(2)}) %copy-start.1) | copy-done | bytes 131096
  2.5 0.0 copy-start.2
  2.5 0.8 copy-done.2
  3.3 0.0 copy-start.3
  3.3 0.8 copy-done.3
  4.2 0.0 copy-start.4
  4.2 0.8 copy-done.4
  5.0 0.0 copy-start.5
  5.0 0.8 copy-done.5
  5.8 81.9 %bounds.1 = (f32[2,64,256]{2,1,0:T(8,128)S(1)}, f32[2,64,256]{2,1,0:T(8,128)S(1)}, f32[256,512]{1,0:T(8,128)S(1)}) custom-call(bf16[2,64,256]{2,1,0:T(8,128)(2,1)S(1)} %bitcast.8, bf16[2,64,256]{2,1,0:T(8,128)(2,1)S(1)} %bitcast.9, bf16[64,512]{1,0:T(8,128)(2,1)S(1)} %copy-done.4, bf16[64,512]{1,0:T(8,128)(2,1)S(1)} %copy-done.5, ...), custom_call_target="tpu_custom_call" | custom-call | flops 2147483648 | bytes 2097152 | tf_op jit(solution)/shard_map/bounds/pallas_call | solution.py:293
  87.8 0.7 copy.12
  88.4 0.7 copy.13
  89.1 0.8 copy.14
Async XLA Ops:
  0.6 1.0 %copy-start = (bf16[256,512]{1,0:T(8,128)(2,1)S(1)}, bf16[256,512]{1,0:T(8,128)(2,1)}, u32[]{:S(2)}) copy-start(bf16[256,512]{1,0:T(8,128)(2,1)} %w.1) | copy-start | bytes 786436
  1.6 0.9 %copy-start.1 = (s32[128,256]{1,0:T(8,128)S(1)}, s32[128,256]{1,0:T(8,128)}, u32[]{:S(2)}) copy-start(s32[128,256]{1,0:T(8,128)} %param.11) | copy-start | bytes 393220
  2.5 0.8 copy-start.2
  3.3 0.8 copy-start.3
  4.2 0.8 copy-start.4
  5.0 0.8 copy-start.5

commit v2 on v1

v2 whole, which is shorter than its diff:
```python
import functools

import jax
import jax.numpy as jnp
from jax import lax
from jax.experimental import pallas as pl
from jax.experimental.pallas import tpu as pltpu
from jax.sharding import PartitionSpec as P

MESH = pl.DeviceIdType.MESH
F32 = jnp.float32
BF16 = jnp.bfloat16


def dot_nt(a, b):
    return lax.dot_general(a, b, (((1,), (1,)), ((), ())), preferred_element_type=F32)


def dot_tn(a, b):
    return lax.dot_general(a, b, (((0,), (0,)), ((), ())), preferred_element_type=F32)


def code(parts, out):
    ups = []
    for i, p in enumerate(parts):
        top = jnp.maximum(jnp.max(jnp.abs(p), axis=0, keepdims=True), 2.0 ** -100)
        e = jnp.floor(jnp.log2(top)) + 1.0
        q = jnp.clip(jnp.round(p * (jnp.exp2(-e) * 32767.0)), -32767.0, 32767.0)
        out[i * 32:(i + 1) * 32] = q.astype(jnp.int32).astype(jnp.int16)
        ups.append(jnp.broadcast_to(e.astype(jnp.int32), (16 // len(parts), 256)))
    out[len(parts) * 32:len(parts) * 32 + 16] = jnp.concatenate(ups, axis=0).astype(jnp.int16)


def decode(src, i, n):
    e = src[n * 32:n * 32 + 16].astype(jnp.int32)[i * (16 // n):i * (16 // n) + 1].astype(F32)
    return src[i * 32:(i + 1) * 32].astype(jnp.int32).astype(F32) * (jnp.exp2(e) * (1.0 / 32767.0))


def kernel(
    scale,
    ctr, rad, gc, gr, w, act,
    oc, orad, ow,
    G, C, Wb, Wa, S, R, Zs, F, acc, wsend, wrecv, gate,
    loc_s, ring_s, ring_r, own_s, own_r, z_s, z_r, sib_s, sib_r, cin_s, cin_r, x_s, x_r, f_s, f_r, ready,
):
    row, col = lax.axis_index("row"), lax.axis_index("col")
    zl, y = row // 8, row % 8
    zh, x, k = col // 8, (col % 8) // 2, col % 2
    z1, z0 = zl // 2, zl % 2
    mid = (z0 + z1) % 2
    ok, fz = 1 - k, 1 - zh
    up, down = (y + 1) % 8, (y + 7) % 8

    def dev(x=x, y=y, zl=zl, zh=zh, k=k):
        return (zl * 8 + y, zh * 8 + x * 2 + k)

    def flip(j):
        return ((z1 + j // 2) % 2) * 2 + (z0 + j % 2) % 2

    order = [0, 1, 2 + mid, 3 - mid]

    def z_of(pair, i):
        return pair * 2 + (z0 + i + mid * ((pair + z1) % 2)) % 2

    def rows32(i):
        return pl.ds(pl.multiple_of(i * 32, 32), 32)

    def rows64(i):
        return pl.ds(pl.multiple_of(i * 64, 64), 64)

    def at_y(off):
        return (y + off + 8) % 8

    sent = []

    def copy(src, dst, ssem, rsem, to):
        return pltpu.make_async_remote_copy(
            src_ref=src, dst_ref=dst, send_sem=ssem, recv_sem=rsem, device_id=to, device_id_type=MESH
        )

    def send(c, cond=None):
        if cond is None:
            c.start()
        else:
            pl.when(cond)(c.start)
        sent.append((c, cond))

    flying = [[], []]

    def send_y(c, i):
        c.start()
        flying[i].append(c)

    zrows = rows32(zl)
    cz = rows32(zh * 2 + x // 2)
    cy = (x % 2) * 4 + k * 2
    local = [
        pltpu.make_async_copy(src, dst, loc_s.at[i])
        for i, (src, dst) in enumerate((
            (gc.at[rows32(k)], G.at[y, 0, k, zrows]),
            (gr.at[rows32(k)], G.at[y, 1, k, zrows]),
            (w, Wb.at[k]),
            (ctr.at[:, rows32(k)], C.at[pl.ds(cy, 2), 0, cz]),
            (rad.at[:, rows32(k)], C.at[pl.ds(cy, 2), 1, cz]),
            (act, gate),
        ))
    ]
    for c in local:
        c.start()

    peers = [dev(y=up), dev(y=down), dev(k=ok)]
    peers += [dev(zl=flip(j)) for j in (1, 2, 3)]
    peers += [dev(x=(x + i) % 4, k=c) for i in (1, 2, 3) for c in (0, 1)]
    partner = dev(zh=fz)
    bar = pltpu.get_barrier_semaphore()
    for p in peers:
        pl.semaphore_signal(bar, inc=1, device_id=p, device_id_type=MESH)

    @pl.when(zh == 0)
    def _():
        pl.semaphore_signal(bar, inc=1, device_id=partner, device_id_type=MESH)
        pl.semaphore_wait(bar, len(peers))

    @pl.when(zh == 1)
    def _():
        pl.semaphore_wait(bar, len(peers) + 1)
        pl.semaphore_signal(ready, inc=1, device_id=partner, device_id_type=MESH)

    local[0].wait()
    local[1].wait()

    def own_y(part, kc):
        blk = G.at[y, :, kc, zrows]
        for i, to in enumerate((up, down)):
            send_y(copy(blk, blk, own_s.at[part, i], own_r.at[part, i], dev(y=to)), i)

    def own_z(part, kc):
        blk = G.at[y, :, kc, zrows]
        for i in (1, 2, 3):
            send(copy(blk, blk, z_s.at[part, i - 1], z_r.at[part, zl], dev(zl=flip(order[i]))))

    sib = dev(k=ok)
    gsib = [copy(ref.at[rows32(ok)], G.at[y, a, k, zrows], sib_s.at[a], sib_r.at[a], sib) for a, ref in enumerate((gc, gr))]
    csib = [
        copy(ref.at[:, rows32(ok)], C.at[pl.ds(cy, 2), a, cz], sib_s.at[2 + a], sib_r.at[2 + a], sib)
        for a, ref in enumerate((ctr, rad))
    ]
    wsib = copy(w, Wb.at[k], sib_s.at[4], sib_r.at[4], sib)
    for c in gsib:
        send(c)
    own_y(0, k)
    own_z(0, k)
    for c in gsib:
        c.wait_recv()
    own_y(1, ok)
    own_z(1, ok)
    for c in csib:
        send(c)
    send(wsib)

    def cin(h):
        return C.at[pl.ds((x % 2) * 4, 4), :, rows32(h * 2 + x // 2)]

    def cin_x(h, part):
        for i in (1, 2, 3):
            send(copy(cin(h), cin(h), cin_s.at[part, i - 1], cin_r.at[part, i - 1], dev(x=(x + i) % 4)))

    far = copy(cin(zh), cin(zh), cin_s.at[2, 0], cin_r.at[2, 0], partner)

    def ring_copy(zs, d, i):
        ys = at_y(d if i else -d)
        if d < 3:
            blk = G.at[ys, :, :, rows32(zs)]
        else:
            blk = G.at[ys, i, :, rows32(zs)]
        return copy(blk, blk, ring_s.at[i, d, zs], ring_r.at[i, d, zs], dev(y=down if i else up))

    def arrive(pair, i, d):
        zs = z_of(pair, i)
        if d == 0:
            for part in (0, 1):
                blk = G.at[y, :, k, rows32(zs)]
                copy(blk, blk, z_s.at[part, 0], z_r.at[part, zs], dev()).wait_recv()
        else:
            for j in (0, 1):
                ring_copy(zs, d - 1, j).wait_recv()

    def step(pair, i, d):
        arrive(pair, i, d)
        if d < 4:
            for j in (0, 1):
                send_y(ring_copy(z_of(pair, i), d, j), j)

    def x_copy(yb, h, g):
        xd, kd = g * 2 + yb // 4, (yb % 4) // 2
        c = copy(S.at[yb, h, g], R.at[x, k, yb % 2, h], x_s.at[yb, h, g], x_r.at[x, k, yb % 2, h], dev(x=xd, k=kd))
        return c, (xd == x) & (kd == k)

    def through(off, h):
        yb = at_y(off)
        p = [dot_nt(G[yb, a, 0, rows64(h)], m[0]) + dot_nt(G[yb, a, 1, rows64(h)], m[1]) for a, m in ((0, Wb), (1, Wa))]
        for g in (0, 1):
            code([t[g * 32:(g + 1) * 32] for t in p], S.at[yb, h, g])
        for g in (0, 1):
            c, here = x_copy(yb, h, g)
            send(c, jnp.logical_not(here))

            @pl.when(here)
            def _():
                R[x, k, yb % 2, h] = S[yb, h, g]

    def grad(blocks, first=False):
        for a in (0, 1):
            for kc in (0, 1):
                t = None
                for off, rows in blocks:
                    yb = at_y(off)
                    if rows is None:
                        p = dot_tn(C[yb, a], G[yb, a, kc])
                    else:
                        p = dot_tn(C[yb, a, rows64(rows)], G[yb, a, kc, rows64(rows)])
                    t = p if t is None else t + p
                if first:
                    acc[a, kc] = t
                else:
                    acc[a, kc] += t

    def arrived(h, yy):
        for i in range(4):
            for kk in (0, 1):
                xs = (x + i) % 4
                c = copy(S.at[0, 0, 0], R.at[xs, kk, yy, h], x_s.at[0, 0, 0], x_r.at[xs, kk, yy, h], dev())
                if i:
                    c.wait_recv()
                else:
                    pl.when(k != kk)(c.wait_recv)

    def total(h, yy, kk, a):
        r = [decode(R.at[i, kk, yy, h], a, 2) for i in range(4)]
        return (r[0] + r[1]) + (r[2] + r[3])

    def z_copy(yy):
        return copy(Zs.at[yy], F.at[yy], f_s.at[yy], f_r.at[yy], partner)

    P_, Q_ = z1, 1 - z1
    step(P_, 1, 0)
    def step_own():
        for part in (0, 1):
            for i in (0, 1):
                blk = G.at[y, :, k, zrows]
                copy(blk, blk, own_s.at[part, i], own_r.at[part, i], dev()).wait_recv()
        for j in (0, 1):
            send_y(ring_copy(zl, 1, j), j)

    step_own()
    step(Q_, 0, 0)
    step(P_, 1, 1)
    step(Q_, 1, 0)
    local[3].wait()
    local[4].wait()
    for c in csib:
        c.wait_recv()

    @pl.when(zh == 0)
    def _():
        pl.semaphore_wait(ready, 1)

    send(far)
    cin_x(zh, 0)
    local[2].wait()
    Wa[k] = jnp.abs(Wb[k])
    wsib.wait_recv()
    Wa[ok] = jnp.abs(Wb[ok])
    through(0, 0)
    through(0, 1)
    step(Q_, 0, 1)
    step(Q_, 1, 1)
    for off in (1, -1):
        for h in (0, 1):
            through(off, h)
    step(fz, 0, 2)
    step(fz, 1, 2)
    far_in = copy(cin(fz), cin(fz), cin_s.at[2, 0], cin_r.at[2, 0], dev())
    far_in.wait_recv()
    cin_x(fz, 1)
    through(2, fz)
    through(-2, fz)
    step(fz, 0, 3)
    step(fz, 1, 3)
    through(3, fz)
    through(-3, fz)
    step(zh, 0, 2)
    for part, h in ((0, zh), (1, fz)):
        for i in (1, 2, 3):
            copy(cin(h), cin(h), cin_s.at[part, i - 1], cin_r.at[part, i - 1], dev()).wait_recv()
    grad([(0, None)], True)
    step(fz, 0, 4)
    step(fz, 1, 4)
    through(4, fz)
    step(zh, 1, 2)
    through(2, zh)
    through(-2, zh)
    grad([(1, None), (-1, None)])
    step(zh, 0, 3)
    step(zh, 1, 3)
    through(3, zh)
    through(-3, zh)
    grad([(2, None), (-2, None)])
    for yy in (0, 1):
        arrived(fz, yy)
        code([total(fz, yy, kk, a) for kk in (0, 1) for a in (0, 1)], Zs.at[yy])
        send(z_copy(yy))
    grad([(3, None), (-3, None), (4, fz)])
    step(zh, 0, 4)
    step(zh, 1, 4)
    through(4, zh)
    grad([(4, zh)])

    def combined(kc):
        wf = Wb[kc].astype(F32)
        sgn = jnp.where(wf > 0, 1.0, jnp.where(wf < 0, -1.0, 0.0))
        return acc[0, kc] + sgn * acc[1, kc]

    wsend[...] = combined(ok)
    wg = copy(wsend, wrecv, sib_s.at[5], sib_r.at[5], sib)
    send(wg)
    ow[...] = combined(k)
    local[5].wait()
    for yy in (0, 1):
        z_copy(yy).wait_recv()
        arrived(zh, yy)
        for kk in (0, 1):
            rows = pl.ds(kk * 32, 32)
            g = gate[yy, rows].astype(F32)
            for a, o in ((0, oc), (1, orad)):
                o[yy, rows] = g * (total(zh, yy, kk, a) + decode(F.at[yy], kk * 2 + a, 4))
    wg.wait_recv()
    ow[...] = (ow[...] + wrecv[...]) * scale
    for c in flying[0] + flying[1]:
        c.wait_send()
    for c, cond in sent:
        if cond is None:
            c.wait_send()
        else:
            pl.when(cond)(c.wait_send)


def on_device(center, radius, grad_center, grad_radius, weight, active):
    hbm = pl.BlockSpec(memory_space=pl.ANY)
    vm = pl.BlockSpec(memory_space=pltpu.VMEM)
    dma = pltpu.SemaphoreType.DMA
    oc, orad, ow = pl.pallas_call(
        functools.partial(kernel, 2048.0 ** -0.5),
        out_shape=(
            jax.ShapeDtypeStruct((2, 64, 256), F32),
            jax.ShapeDtypeStruct((2, 64, 256), F32),
            jax.ShapeDtypeStruct((256, 512), F32),
        ),
        in_specs=[hbm] * 6,
        out_specs=(vm,) * 3,
        scratch_shapes=[
            pltpu.VMEM((8, 2, 2, 128, 512), BF16),
            pltpu.VMEM((8, 2, 128, 256), BF16),
            pltpu.VMEM((2, 256, 512), BF16),
            pltpu.VMEM((2, 256, 512), BF16),
            pltpu.VMEM((8, 2, 2, 80, 256), jnp.int16),
            pltpu.VMEM((4, 2, 2, 2, 80, 256), jnp.int16),
            pltpu.VMEM((2, 144, 256), jnp.int16),
            pltpu.VMEM((2, 144, 256), jnp.int16),
            pltpu.VMEM((2, 2, 256, 512), F32),
            pltpu.VMEM((256, 512), F32),
            pltpu.VMEM((256, 512), F32),
            pltpu.VMEM((2, 64, 256), jnp.int32),
            dma((6,)),
            dma((2, 4, 4)), dma((2, 4, 4)),
            dma((2, 2)), dma((2, 2)),
            dma((2, 3)), dma((2, 4)),
            dma((6,)), dma((6,)),
            dma((3, 3)), dma((3, 3)),
            dma((8, 2, 2)), dma((4, 2, 2, 2)),
            dma((2,)), dma((2,)),
            pltpu.SemaphoreType.REGULAR,
        ],
        compiler_params=pltpu.CompilerParams(collective_id=0, has_side_effects=True, vmem_limit_bytes=48 * 2**20),
        cost_estimate=pl.CostEstimate(flops=2 * 2**30, bytes_accessed=2**21, transcendentals=0),
        name="bounds",
    )(
        *[pltpu.with_memory_space_constraint(v, pltpu.HBM) for v in (
            center.reshape(2, 64, 256), radius.reshape(2, 64, 256), grad_center, grad_radius, weight, active.reshape(2, 64, 256)
        )]
    )
    return oc.reshape(128, 256), orad.reshape(128, 256), ow


def solution(mesh):
    in_specs = (
        P("col", "row"),
        P("col", "row"),
        P("row", "col"),
        P("row", "col"),
        P("row", "col"),
        P("col", "row"),
    )
    out_specs = (P("col", "row"), P("col", "row"), P("row", "col"))
    return jax.shard_map(
        on_device, mesh=mesh, in_specs=in_specs, out_specs=out_specs, check_vma=False
    )
```

time: 90.2 us -> 72.9 us (0.81)
  the two profiles are of different devices: /device:TPU:10 before, /device:TPU:23 now
where the time goes in v2:
time: 72.9 us; the launch traced here: 72.8 us
  Pallas kernels  70.1 us (96%)
  local copies, waits for them, and re-layouts  2.11 us (3%)
    pallas_call x1, Pallas kernels, on_device(): pl.pallas_call(functools.partial(kernel, 2048.0 ** (-0.5)), out_shape=(ja...  70.1 us
    unnamed x3, local copies, waits for them, and re-layouts  2.11 us

profile of v2, /device:TPU:23, one launch (start us, length us, event | category | flops | bytes accessed | tf_op | source)
XLA Modules:
  0.0 72.8 jit_solution(2671977679872058314)
XLA Ops:
  0.6 70.1 %bounds.1 = (f32[2,64,256]{2,1,0:T(8,128)S(1)}, f32[2,64,256]{2,1,0:T(8,128)S(1)}, f32[256,512]{1,0:T(8,128)S(1)}) custom-call(bf16[2,64,256]{2,1,0:T(8,128)(2,1)} %bitcast.8, bf16[2,64,256]{2,1,0:T(8,128)(2,1)} %bitcast.9, bf16[64,512]{1,0:T(8,128)(2,1)} %gc.1, bf16[64,512]{1,0:T(8,128)(2,1)} %gr.1, bf16[256,512]{1,0:T(8,128)(2,1)} %w.1, s32[2,64,256]{2,1,0:T(8,128)} %bitcast.7), custom_call_target="tpu_custom_call" | custom-call | flops 2147483648 | bytes 2097152 | tf_op jit(solution)/shard_map/bounds/pallas_call | solution.py:352
  70.7 0.7 copy.12
  71.3 0.7 copy.13
  72.0 0.8 %copy.14 = f32[256,512]{1,0:T(8,128)} copy(f32[256,512]{1,0:T(8,128)S(1)} %get-tuple-element.14) | data formatting | bytes 1048576

commit v3 on v2

--- a/solution.py
+++ b/solution.py
@@ -186,6 +186,16 @@
                 ring_copy(zs, d - 1, j).wait_recv()
 
     def step(pair, i, d):
+        if d == 1 and i == 0:
+            @pl.when(pair != z1)
+            def _():
+                arrive(pair, i, d)
+                for j in (0, 1):
+                    ring_copy(z_of(pair, i), d, j).start()
+
+            for j in (0, 1):
+                sent.append((ring_copy(z_of(pair, i), d, j), pair != z1))
+            return
         arrive(pair, i, d)
         if d < 4:
             for j in (0, 1):
@@ -209,9 +219,9 @@
             def _():
                 R[x, k, yb % 2, h] = S[yb, h, g]
 
-    def grad(blocks, first=False):
-        for a in (0, 1):
-            for kc in (0, 1):
+    def grad(blocks, first=False, columns=(0, 1)):
+        for kc in columns:
+            for a in (0, 1):
                 t = None
                 for off, rows in blocks:
                     yb = at_y(off)
@@ -243,7 +253,7 @@
         return copy(Zs.at[yy], F.at[yy], f_s.at[yy], f_r.at[yy], partner)
 
     P_, Q_ = z1, 1 - z1
-    step(P_, 1, 0)
+
     def step_own():
         for part in (0, 1):
             for i in (0, 1):
@@ -253,77 +263,79 @@
             send_y(ring_copy(zl, 1, j), j)
 
     step_own()
+    step(P_, 1, 0)
     step(Q_, 0, 0)
-    step(P_, 1, 1)
     step(Q_, 1, 0)
-    local[3].wait()
-    local[4].wait()
-    for c in csib:
-        c.wait_recv()
-
-    @pl.when(zh == 0)
-    def _():
-        pl.semaphore_wait(ready, 1)
-
-    send(far)
-    cin_x(zh, 0)
     local[2].wait()
     Wa[k] = jnp.abs(Wb[k])
     wsib.wait_recv()
     Wa[ok] = jnp.abs(Wb[ok])
     through(0, 0)
     through(0, 1)
-    step(Q_, 0, 1)
-    step(Q_, 1, 1)
-    for off in (1, -1):
-        for h in (0, 1):
-            through(off, h)
+    def both(i, h):
+        through(i, h)
+        through(-i, h)
+
+    step(fz, 0, 1)
+    step(fz, 1, 1)
+    local[3].wait()
+    local[4].wait()
+    for c in csib:
+        c.wait_recv()
+
+    @pl.when(zh == 0)
+    def _():
+        pl.semaphore_wait(ready, 1)
+
+    send(far)
+    cin_x(zh, 0)
+    both(1, fz)
     step(fz, 0, 2)
     step(fz, 1, 2)
+    both(2, fz)
+    step(fz, 0, 3)
+    step(fz, 1, 3)
     far_in = copy(cin(fz), cin(fz), cin_s.at[2, 0], cin_r.at[2, 0], dev())
     far_in.wait_recv()
     cin_x(fz, 1)
-    through(2, fz)
-    through(-2, fz)
-    step(fz, 0, 3)
-    step(fz, 1, 3)
-    through(3, fz)
-    through(-3, fz)
+    both(3, fz)
+    step(zh, 0, 1)
+    step(zh, 1, 1)
+    step(fz, 0, 4)
+    step(fz, 1, 4)
+    through(4, fz)
+    both(1, zh)
     step(zh, 0, 2)
+    step(zh, 1, 2)
+    for yy in (0, 1):
+        arrived(fz, yy)
+        code([total(fz, yy, kk, a) for kk in (0, 1) for a in (0, 1)], Zs.at[yy])
+        send(z_copy(yy))
+    both(2, zh)
     for part, h in ((0, zh), (1, fz)):
         for i in (1, 2, 3):
             copy(cin(h), cin(h), cin_s.at[part, i - 1], cin_r.at[part, i - 1], dev()).wait_recv()
     grad([(0, None)], True)
-    step(fz, 0, 4)
-    step(fz, 1, 4)
-    through(4, fz)
-    step(zh, 1, 2)
-    through(2, zh)
-    through(-2, zh)
     grad([(1, None), (-1, None)])
     step(zh, 0, 3)
     step(zh, 1, 3)
-    through(3, zh)
-    through(-3, zh)
+    both(3, zh)
     grad([(2, None), (-2, None)])
-    for yy in (0, 1):
-        arrived(fz, yy)
-        code([total(fz, yy, kk, a) for kk in (0, 1) for a in (0, 1)], Zs.at[yy])
-        send(z_copy(yy))
     grad([(3, None), (-3, None), (4, fz)])
     step(zh, 0, 4)
     step(zh, 1, 4)
     through(4, zh)
-    grad([(4, zh)])
 
     def combined(kc):
         wf = Wb[kc].astype(F32)
         sgn = jnp.where(wf > 0, 1.0, jnp.where(wf < 0, -1.0, 0.0))
         return acc[0, kc] + sgn * acc[1, kc]
 
+    grad([(4, zh)], columns=(ok,))
     wsend[...] = combined(ok)
     wg = copy(wsend, wrecv, sib_s.at[5], sib_r.at[5], sib)
     send(wg)
+    grad([(4, zh)], columns=(k,))
     ow[...] = combined(k)
     local[5].wait()
     for yy in (0, 1):

time: 72.9 us -> 67.6 us (0.927)
  the two profiles are of different devices: /device:TPU:23 before, /device:TPU:10 now
where the time goes in v3:
time: 67.6 us; the launch traced here: 67.5 us
  Pallas kernels  64.8 us (96%)
  local copies, waits for them, and re-layouts  2.11 us (3%)
    pallas_call x1, Pallas kernels, on_device(): pl.pallas_call(functools.partial(kernel, 2048.0 ** (-0.5)), out_shape=(ja...  64.8 us
    unnamed x3, local copies, waits for them, and re-layouts  2.11 us

profile of v3, /device:TPU:10, one launch (start us, length us, event | category | flops | bytes accessed | tf_op | source)
XLA Modules:
  0.0 67.5 jit_solution(8660905826326650671)
XLA Ops:
  0.6 64.8 %bounds.1 = (f32[2,64,256]{2,1,0:T(8,128)S(1)}, f32[2,64,256]{2,1,0:T(8,128)S(1)}, f32[256,512]{1,0:T(8,128)S(1)}) custom-call(bf16[2,64,256]{2,1,0:T(8,128)(2,1)} %bitcast.8, bf16[2,64,256]{2,1,0:T(8,128)(2,1)} %bitcast.9, bf16[64,512]{1,0:T(8,128)(2,1)} %gc.1, bf16[64,512]{1,0:T(8,128)(2,1)} %gr.1, bf16[256,512]{1,0:T(8,128)(2,1)} %w.1, s32[2,64,256]{2,1,0:T(8,128)} %bitcast.7), custom_call_target="tpu_custom_call" | custom-call | flops 2147483648 | bytes 2097152 | tf_op jit(solution)/shard_map/bounds/pallas_call | solution.py:364
  65.4 0.7 copy.12
  66.1 0.7 copy.13
  66.7 0.8 %copy.14 = f32[256,512]{1,0:T(8,128)} copy(f32[256,512]{1,0:T(8,128)S(1)} %get-tuple-element.14) | data formatting | bytes 1048576

commit v4 on v3

--- a/solution.py
+++ b/solution.py
@@ -167,39 +167,41 @@
 
     far = copy(cin(zh), cin(zh), cin_s.at[2, 0], cin_r.at[2, 0], partner)
 
-    def ring_copy(zs, d, i):
+    def ring_copy(zs, d, i, part):
         ys = at_y(d if i else -d)
-        if d < 3:
-            blk = G.at[ys, :, :, rows32(zs)]
+        kc = ok if part else k
+        blk = G.at[ys, :, kc, rows32(zs)] if d < 3 else G.at[ys, i, kc, rows32(zs)]
+        return copy(blk, blk, ring_s.at[i, d, zs, part], ring_r.at[i, d, zs, part], dev(y=down if i else up))
+
+    def arrive(zs, d, j, part):
+        if d == 0:
+            blk = G.at[y, :, k, rows32(zs)]
+            copy(blk, blk, z_s.at[part, 0], z_r.at[part, zs], dev()).wait_recv()
         else:
-            blk = G.at[ys, i, :, rows32(zs)]
-        return copy(blk, blk, ring_s.at[i, d, zs], ring_r.at[i, d, zs], dev(y=down if i else up))
-
-    def arrive(pair, i, d):
+            ring_copy(zs, d - 1, j, part).wait_recv()
+
+    def pass_on(zs, d):
+        for part in (0, 1):
+            if d == 0:
+                arrive(zs, 0, 0, part)
+            for j in (0, 1):
+                if d:
+                    arrive(zs, d, j, part)
+                if d < 4:
+                    ring_copy(zs, d, j, part).start()
+
+    def step(pair, i, d):
         zs = z_of(pair, i)
-        if d == 0:
+        cond = None
+        if d == 1 and i == 0:
+            cond = pair != z1
+            pl.when(cond)(lambda: pass_on(zs, d))
+        else:
+            pass_on(zs, d)
+        if d < 4:
             for part in (0, 1):
-                blk = G.at[y, :, k, rows32(zs)]
-                copy(blk, blk, z_s.at[part, 0], z_r.at[part, zs], dev()).wait_recv()
-        else:
-            for j in (0, 1):
-                ring_copy(zs, d - 1, j).wait_recv()
-
-    def step(pair, i, d):
-        if d == 1 and i == 0:
-            @pl.when(pair != z1)
-            def _():
-                arrive(pair, i, d)
                 for j in (0, 1):
-                    ring_copy(z_of(pair, i), d, j).start()
-
-            for j in (0, 1):
-                sent.append((ring_copy(z_of(pair, i), d, j), pair != z1))
-            return
-        arrive(pair, i, d)
-        if d < 4:
-            for j in (0, 1):
-                send_y(ring_copy(z_of(pair, i), d, j), j)
+                    sent.append((ring_copy(zs, d, j, part), cond))
 
     def x_copy(yb, h, g):
         xd, kd = g * 2 + yb // 4, (yb % 4) // 2
@@ -218,6 +220,21 @@
             @pl.when(here)
             def _():
                 R[x, k, yb % 2, h] = S[yb, h, g]
+
+    def through_last():
+        yb = at_y(4)
+        for i in (0, 1):
+            step(zh, i, 4)
+            zs = z_of(zh, i)
+            g = zs % 2
+            p = [dot_nt(G[yb, a, 0, rows32(zs)], m[0]) + dot_nt(G[yb, a, 1, rows32(zs)], m[1]) for a, m in ((0, Wb), (1, Wa))]
+            code(p, S.at[yb, zh, g])
+            c, here = x_copy(yb, zh, g)
+            send(c, jnp.logical_not(here))
+
+            @pl.when(here)
+            def _():
+                R[x, k, yb % 2, zh] = S[yb, zh, g]
 
     def grad(blocks, first=False, columns=(0, 1)):
         for kc in columns:
@@ -255,12 +272,11 @@
     P_, Q_ = z1, 1 - z1
 
     def step_own():
+        blk = G.at[y, :, k, zrows]
         for part in (0, 1):
-            for i in (0, 1):
-                blk = G.at[y, :, k, zrows]
-                copy(blk, blk, own_s.at[part, i], own_r.at[part, i], dev()).wait_recv()
-        for j in (0, 1):
-            send_y(ring_copy(zl, 1, j), j)
+            for j in (0, 1):
+                copy(blk, blk, own_s.at[part, j], own_r.at[part, j], dev()).wait_recv()
+                send_y(ring_copy(zl, 1, j, part), j)
 
     step_own()
     step(P_, 1, 0)
@@ -322,9 +338,7 @@
     both(3, zh)
     grad([(2, None), (-2, None)])
     grad([(3, None), (-3, None), (4, fz)])
-    step(zh, 0, 4)
-    step(zh, 1, 4)
-    through(4, zh)
+    through_last()
 
     def combined(kc):
         wf = Wb[kc].astype(F32)
@@ -384,7 +398,7 @@
             pltpu.VMEM((256, 512), F32),
             pltpu.VMEM((2, 64, 256), jnp.int32),
             dma((6,)),
-            dma((2, 4, 4)), dma((2, 4, 4)),
+            dma((2, 4, 4, 2)), dma((2, 4, 4, 2)),
             dma((2, 2)), dma((2, 2)),
             dma((2, 3)), dma((2, 4)),
             dma((6,)), dma((6,)),

time: 67.6 us -> 66.3 us (0.981)
  the two profiles are of different devices: /device:TPU:10 before, /device:TPU:49 now
where the time goes in v4:
time: 66.3 us; the launch traced here: 66.2 us
  Pallas kernels  63.4 us (96%)
  local copies, waits for them, and re-layouts  2.11 us (3%)
    pallas_call x1, Pallas kernels, on_device(): pl.pallas_call(functools.partial(kernel, 2048.0 ** (-0.5)), out_shape=(ja...  63.4 us
    unnamed x3, local copies, waits for them, and re-layouts  2.11 us

profile of v4, /device:TPU:49, one launch (start us, length us, event | category | flops | bytes accessed | tf_op | source)
XLA Modules:
  0.0 66.2 jit_solution(6635423276220444510)
XLA Ops:
  0.6 63.4 %bounds.1 = (f32[2,64,256]{2,1,0:T(8,128)S(1)}, f32[2,64,256]{2,1,0:T(8,128)S(1)}, f32[256,512]{1,0:T(8,128)S(1)}) custom-call(bf16[2,64,256]{2,1,0:T(8,128)(2,1)} %bitcast.8, bf16[2,64,256]{2,1,0:T(8,128)(2,1)} %bitcast.9, bf16[64,512]{1,0:T(8,128)(2,1)} %gc.1, bf16[64,512]{1,0:T(8,128)(2,1)} %gr.1, bf16[256,512]{1,0:T(8,128)(2,1)} %w.1, s32[2,64,256]{2,1,0:T(8,128)} %bitcast.7), custom_call_target="tpu_custom_call" | custom-call | flops 2147483648 | bytes 2097152 | tf_op jit(solution)/shard_map/bounds/pallas_call | solution.py:378
  64.1 0.7 copy.12
  64.7 0.7 copy.13
  65.4 0.8 %copy.14 = f32[256,512]{1,0:T(8,128)} copy(f32[256,512]{1,0:T(8,128)S(1)} %get-tuple-element.14) | data formatting | bytes 1048576

commit v5 on v4

--- a/solution.py
+++ b/solution.py
@@ -286,8 +286,6 @@
     Wa[k] = jnp.abs(Wb[k])
     wsib.wait_recv()
     Wa[ok] = jnp.abs(Wb[ok])
-    through(0, 0)
-    through(0, 1)
     def both(i, h):
         through(i, h)
         through(-i, h)
@@ -305,21 +303,23 @@
 
     send(far)
     cin_x(zh, 0)
+    through(0, fz)
     both(1, fz)
     step(fz, 0, 2)
     step(fz, 1, 2)
     both(2, fz)
+    step(zh, 0, 1)
     step(fz, 0, 3)
     step(fz, 1, 3)
     far_in = copy(cin(fz), cin(fz), cin_s.at[2, 0], cin_r.at[2, 0], dev())
     far_in.wait_recv()
     cin_x(fz, 1)
     both(3, fz)
-    step(zh, 0, 1)
     step(zh, 1, 1)
     step(fz, 0, 4)
     step(fz, 1, 4)
     through(4, fz)
+    through(0, zh)
     both(1, zh)
     step(zh, 0, 2)
     step(zh, 1, 2)

time: 66.3 us -> 66.1 us (level)
  no operation moved by 1% of the time
where the time goes in v5:
time: 66.1 us; the launch traced here: 66 us
  Pallas kernels  63.2 us (96%)
  local copies, waits for them, and re-layouts  2.11 us (3%)
    pallas_call x1, Pallas kernels, on_device(): pl.pallas_call(functools.partial(kernel, 2048.0 ** (-0.5)), out_shape=(ja...  63.2 us
    unnamed x3, local copies, waits for them, and re-layouts  2.11 us

profile of v5, /device:TPU:49, one launch (start us, length us, event | category | flops | bytes accessed | tf_op | source)
XLA Modules:
  0.0 66.0 jit_solution(15755299928518999748)
XLA Ops:
  0.6 63.2 %bounds.1 = (f32[2,64,256]{2,1,0:T(8,128)S(1)}, f32[2,64,256]{2,1,0:T(8,128)S(1)}, f32[256,512]{1,0:T(8,128)S(1)}) custom-call(bf16[2,64,256]{2,1,0:T(8,128)(2,1)} %bitcast.8, bf16[2,64,256]{2,1,0:T(8,128)(2,1)} %bitcast.9, bf16[64,512]{1,0:T(8,128)(2,1)} %gc.1, bf16[64,512]{1,0:T(8,128)(2,1)} %gr.1, bf16[256,512]{1,0:T(8,128)(2,1)} %w.1, s32[2,64,256]{2,1,0:T(8,128)} %bitcast.7), custom_call_target="tpu_custom_call" | custom-call | flops 2147483648 | bytes 2097152 | tf_op jit(solution)/shard_map/bounds/pallas_call | solution.py:378
  63.9 0.7 copy.12
  64.5 0.7 copy.13
  65.2 0.8 %copy.14 = f32[256,512]{1,0:T(8,128)} copy(f32[256,512]{1,0:T(8,128)S(1)} %get-tuple-element.14) | data formatting | bytes 1048576
